TPU v7x, 1024 devices: a whole 8x8x8 slice. The times are simulated.
1024 devices in a mesh: member: 64 (over x, y_lo, core), lat: 16 (over z, y_hi).
Axes of the slice: x: 8, y: 8 (y_hi: 2, y_lo: 4; y = y_hi * 4 + y_lo), z: 8, core: 2. Of those that a mesh axis runs over, the one named last changes fastest.
Arguments:
- state: float32 [256, 128, 8, 256], P('member', 'lat'), may hold values from -6 to 6
- zonal_wind: float32 [128, 8, 256], P('lat'), may hold values from -5 to 5
- meridional_wind: float32 [128, 8, 256], P('lat'), may hold values from -5 to 5
- obs_cell: int32 [128, 8, 128], P('lat'), may hold values from 0 to 255
- obs_value: float32 [128, 8, 128], P('lat'), may hold values from -10 to 10
- obs_weight: float32 [128, 8, 128], P('lat'), may hold values from 1 to 1024
Outputs:
- analysis: float32 [256, 128, 8, 256], P('member', 'lat')
All inputs are finite; a program needn't handle non-finite values.
Results may differ from a plain program's by a relative error of at most 0.00014.
Values sent between devices are 32-bit elements; how exact they have to be, the bound alone decides.
A program may use at most 32 MiB of HBM per device.

v0:
```python
import jax
import jax.numpy as jnp
from jax import lax
from jax.sharding import PartitionSpec as P

SWEEPS = 3


step_size = 0.3


def extended(block, sides, width):
    for axis, dim in sides:
        count = lax.axis_size(axis)
        forward = [(i, i + 1) for i in range(count - 1)]
        backward = [(target, source) for source, target in forward]
        low = lax.ppermute(
            lax.slice_in_dim(block, block.shape[dim] - width, None, axis=dim), axis, forward
        )
        high = lax.ppermute(lax.slice_in_dim(block, 0, width, axis=dim), axis, backward)
        block = jnp.concatenate([low, block, high], axis=dim)
    return block


def advance(padded, zonal, meridional):
    middle = padded[:, 1:-1]
    north_row = padded[:, 2:]
    south_row = padded[:, :-2]
    east_cell = jnp.roll(middle, -1, axis=3)
    west_cell = jnp.roll(middle, 1, axis=3)
    return middle - step_size * (
        (zonal + middle) * (east_cell - west_cell) * 0.5
        + meridional * (north_row - south_row) * 0.5
    )


def analyse(ensemble, observed, values, weights):
    highest = lax.Precision.HIGHEST
    count = ensemble.shape[0]
    obs_mean = jnp.mean(observed, axis=0)
    perturb = observed - obs_mean
    innovation = values - obs_mean
    gram = jnp.einsum("kro,lro->rkl", perturb * weights, perturb, precision=highest)
    identity = jnp.eye(count, dtype=jnp.float32)
    system = gram + (count - 1.0) * identity
    frobenius = jnp.sqrt(jnp.sum(system * system, axis=(1, 2)))
    iterate = system / frobenius[:, None, None]
    inverse = jnp.broadcast_to(identity, system.shape)
    for sweep in range(SWEEPS):
        product = jnp.einsum("rij,rjk->rik", inverse, iterate, precision=highest)
        factor = 1.5 * identity - 0.5 * product
        iterate = jnp.einsum("rij,rjk->rik", iterate, factor, precision=highest)
        inverse = jnp.einsum("rij,rjk->rik", factor, inverse, precision=highest)
    root = inverse / jnp.sqrt(frobenius)[:, None, None]
    covariance = jnp.einsum("rij,rjk->rik", root, root, precision=highest)
    projected = jnp.einsum("kro,ro->rk", perturb, weights * innovation, precision=highest)
    mean_weights = jnp.einsum("rkl,rl->rk", covariance, projected, precision=highest)
    transform = mean_weights[:, :, None] + jnp.sqrt(count - 1.0) * root
    state_mean = jnp.mean(ensemble, axis=0)
    state_pert = ensemble - state_mean
    return state_mean + jnp.einsum("rkm,krn->mrn", transform, state_pert, precision=highest)


def pick_columns(rows, cells):
    return jax.vmap(
        lambda block, index: jnp.take(block, index, axis=1), in_axes=(1, 0), out_axes=1
    )(rows, cells)


def with_rim(field):
    return extended(field, (("lat", 1),), 1)


def body(state, zonal_wind, meridional_wind, obs_cell, obs_value, obs_weight):
    members_dev, lat_dev, levels, longitudes = state.shape
    groups = lax.axis_size("member")
    regions = lat_dev * levels // groups
    count = members_dev * groups
    field = state
    for iteration in range(2):
        field = advance(with_rim(field), zonal_wind, meridional_wind)
    flat = field.reshape(members_dev, lat_dev * levels, longitudes)
    all_cells = obs_cell.reshape(lat_dev * levels, -1)
    start = lax.axis_index("member") * regions
    cells = lax.dynamic_slice_in_dim(all_cells, start, regions, 0)
    values = lax.dynamic_slice_in_dim(obs_value.reshape(lat_dev * levels, -1), start, regions, 0)
    weights = lax.dynamic_slice_in_dim(obs_weight.reshape(lat_dev * levels, -1), start, regions, 0)
    ensemble = lax.all_to_all(
        flat.reshape(members_dev, groups, regions, longitudes),
        "member",
        split_axis=1,
        concat_axis=0,
        tiled=True,
    ).reshape(count, regions, longitudes)
    observed = pick_columns(ensemble, cells)
    analysed = analyse(ensemble, observed, values, weights)
    returned = lax.all_to_all(
        analysed.reshape(count, 1, regions, longitudes),
        "member",
        split_axis=0,
        concat_axis=1,
        tiled=True,
    )
    return returned.reshape(state.shape)


def solution(mesh):
    in_specs = (
        P("member", "lat", None, None),
        P("lat", None, None),
        P("lat", None, None),
        P("lat", None, None),
        P("lat", None, None),
        P("lat", None, None),
    )
    out_specs = P("member", "lat", None, None)
    return jax.shard_map(body, mesh=mesh, in_specs=in_specs, out_specs=out_specs, check_vma=False)
```

profile of v0, /device:TPU:129, one launch (start us, length us, event | category | flops | bytes accessed | tf_op | source)
XLA Modules:
  0.0 88.3 jit_solution(14916096231880316527)
XLA Ops:
  0.0 0.8 fusion.51
  0.8 6.1 %collective-permute-start = (f32[4,1,8,256]{3,2,1,0:T(8,128)S(1)}, f32[4,1,8,256]{3,2,1,0:T(8,128)S(1)}, u32[]{:S(2)}, u32[]{:S(2)}) collective-permute-start(f32[4,1,8,256]{3,2,1,0:T(8,128)S(1)} %get-tuple-element.17), channel_id=1, source_target_pairs={{1,0},{2,1},{3,2},{4,3},{5,4},{6,5},{7,6},{8,7},{9,8},{10,9},{11,1... | collective-permute-start | bytes 98312 | tf_op jit(solution)/shard_map/ppermute | solution.py:20
  6.9 0.0 copy-start
  6.9 3.9 %collective-permute-start.1 = (f32[4,1,8,256]{3,2,1,0:T(8,128)S(1)}, f32[4,1,8,256]{3,2,1,0:T(8,128)S(1)}, u32[]{:S(2)}, u32[]{:S(2)}) collective-permute-start(f32[4,1,8,256]{3,2,1,0:T(8,128)S(1)} %get-tuple-element.18), channel_id=1, source_target_pairs={{0,1},{1,2},{2,3},{3,4},{4,5},{5,6},{6,7},{7,8},{8,9},{9,10},{10,1... | collective-permute-start | bytes 98312 | tf_op jit(solution)/shard_map/ppermute | solution.py:17
  10.8 1.2 %fusion.50 = (f32[4,8,8,255]{3,2,1,0:T(8,128)S(1)}, f32[4,8,8,255]{3,2,1,0:T(8,128)S(1)}) fusion(f32[4,8,8,256]{3,2,1,0:T(8,128)} %param.6), kind=kLoop, calls=%fused_computation.77 | loop fusion | bytes 1044480 | tf_op jit(solution)/shard_map/jit(_roll_static)/slice | solution.py:30
  11.9 0.0 copy-done
  11.9 0.0 copy-start.1
  11.9 0.0 copy-start.2
  12.0 0.1 fusion.49
  12.1 0.0 collective-permute-done
  12.1 4.8 %collective-permute-done.1 = f32[4,1,8,256]{3,2,1,0:T(8,128)S(1)} collective-permute-done((f32[4,1,8,256]{3,2,1,0:T(8,128)S(1)}, f32[4,1,8,256]{3,2,1,0:T(8,128)S(1)}, u32[]{:S(2)}, u32[]{:S(2)}) %collective-permute-start.1) | collective-permute-done | bytes 32800 | tf_op jit(solution)/shard_map/ppermute | solution.py:17
  16.8 0.0 copy-done.1
  16.8 0.0 copy-done.2
  16.8 0.2 fusion.14
  17.0 0.1 fusion.47
  17.2 2.3 %collective-permute-start.2 = (f32[4,1,8,256]{3,2,1,0:T(8,128)S(1)}, f32[4,1,8,256]{3,2,1,0:T(8,128)S(1)}, u32[]{:S(2)}, u32[]{:S(2)}) collective-permute-start(f32[4,1,8,256]{3,2,1,0:T(8,128)S(1)} %get-tuple-element.11), channel_id=1, source_target_pairs={{1,0},{2,1},{3,2},{4,3},{5,4},{6,5},{7,6},{8,7},{9,8},{10,9},{11,1... | collective-permute-start | bytes 98312 | tf_op jit(solution)/shard_map/ppermute | solution.py:20
  19.5 6.9 %collective-permute-start.3 = (f32[4,1,8,256]{3,2,1,0:T(8,128)S(1)}, f32[4,1,8,256]{3,2,1,0:T(8,128)S(1)}, u32[]{:S(2)}, u32[]{:S(2)}) collective-permute-start(f32[4,1,8,256]{3,2,1,0:T(8,128)S(1)} %get-tuple-element.12), channel_id=1, source_target_pairs={{0,1},{1,2},{2,3},{3,4},{4,5},{5,6},{6,7},{7,8},{8,9},{9,10},{10,1... | collective-permute-start | bytes 98312 | tf_op jit(solution)/shard_map/ppermute | solution.py:17
  26.4 0.1 fusion.46
  26.5 0.0 collective-permute-done.2
  26.5 2.7 %collective-permute-done.3 = f32[4,1,8,256]{3,2,1,0:T(8,128)S(1)} collective-permute-done((f32[4,1,8,256]{3,2,1,0:T(8,128)S(1)}, f32[4,1,8,256]{3,2,1,0:T(8,128)S(1)}, u32[]{:S(2)}, u32[]{:S(2)}) %collective-permute-start.3) | collective-permute-done | bytes 32800 | tf_op jit(solution)/shard_map/ppermute | solution.py:17
  29.2 0.2 fusion.9
  29.4 0.9 copy.13
  30.3 17.8 %all-to-all-start = ((f32[4,64,1,256]{3,0,2,1:T(4,128)}), f32[4,64,1,256]{3,0,2,1:T(4,128)S(1)}, u32[]{:S(2)}, u32[]{:S(2)}) async-start(f32[4,64,1,256]{3,0,2,1:T(4,128)} %bitcast), calls=%async_computation | async-start | bytes 524288 | tf_op jit(solution)/shard_map/all_to_all | solution.py:88
  48.1 0.7 and_bitcast_fusion
  48.8 0.7 fusion.42
  49.5 11.3 %all-to-all-done = f32[4,64,1,256]{3,0,2,1:T(4,128)S(1)} async-done(((f32[4,64,1,256]{3,0,2,1:T(4,128)}), f32[4,64,1,256]{3,0,2,1:T(4,128)S(1)}, u32[]{:S(2)}, u32[]{:S(2)}) %all-to-all-start) | async-done | bytes 262176 | tf_op jit(solution)/shard_map/all_to_all | solution.py:88
  60.8 0.3 transpose.18
  61.1 0.1 copy.14
  61.3 1.0 %gather_fusion = f32[128,256]{1,0:T(8,128)S(1)} fusion(f32[1,256,256]{1,2,0:T(8,128)S(1)} %copy.14, s32[128]{0:T(128)S(1)} %or_bitcast_fusion), kind=kCustom, calls=%fused_computation | custom fusion | bytes 263168 | tf_op jit(solution)/shard_map/vmap(jit(_take))/gather | solution.py:66
  62.3 0.2 fusion.24
  62.5 1.1 %multiply_reduce_fusion = (f32[]{:T(128)}, f32[256,256]{1,0:T(8,128)S(1)}) fusion(f32[128,256]{1,0:T(8,128)S(1)} %gather_fusion, f32[128]{0:T(128)S(1)} %broadcast_multiply_fusion.1, pred[128]{0:T(512)(128)(4,1)S(1)} %get-tuple-element.5, f32[128]{0:T(128)S(1)} %fusion.42), kind=kOutput, calls=%fused_computation.34 | convolution fusion | flops 101154816 | bytes 394372 | tf_op jit(solution)/shard_map/kro,lro->rkl/dot_general | solution.py:43
  64.3 0.3 fusion.2
  64.6 0.4 fusion.30
  65.0 0.3 fusion.19
  65.3 0.4 fusion.1
  65.7 0.4 fusion.53
  66.1 0.4 fusion.52
  66.5 1.0 %convolution_bitcast_fusion.1 = f32[256,1]{0,1:T(1,128)S(1)} fusion(f32[128,256]{1,0:T(8,128)S(1)} %gather_fusion, f32[128]{0:T(128)S(1)} %broadcast_multiply_fusion.1, pred[128]{0:T(512)(128)(4,1)S(1)} %get-tuple-element.5, f32[64,128]{1,0:T(8,128)} %bitcast.106, s32[]{:T(128)S(6)} %select_n.53, f32[64,128]{1,0:T(8,128)} %bitcast.105), kind=kOutput, calls=%fused_computation.12 | convolution fusion | flops 459008 | bytes 134660 | tf_op jit(solution)/shard_map/kro,ro->rk/dot_general | solution.py:56
  67.5 0.4 fusion
  67.9 0.4 convolution_divide_fusion
  68.3 0.4 fusion.54
  68.6 0.1 reduce_sum.27
  68.8 0.1 sub.95
  68.9 0.3 fusion.55
  69.2 0.7 fusion.4
  69.9 0.2 copy.15
  70.1 17.5 %all_to_all.30 = f32[256,1,1,256]{3,2,1,0:T(1,128)S(1)} all-to-all(f32[256,1,1,256]{3,2,1,0:T(1,128)S(1)} %copy.15), channel_id=1, replica_groups=mesh['member'=64,'lat'=16] {'member'}, dimensions={0} | all-to-all | bytes 524288 | tf_op jit(solution)/shard_map/all_to_all | solution.py:97
  87.5 0.8 copy.19
  (6 shorter events, 0.1 us)
Async XLA Ops:
  0.8 11.3 %collective-permute-start = (f32[4,1,8,256]{3,2,1,0:T(8,128)S(1)}, f32[4,1,8,256]{3,2,1,0:T(8,128)S(1)}, u32[]{:S(2)}, u32[]{:S(2)}) collective-permute-start(f32[4,1,8,256]{3,2,1,0:T(8,128)S(1)} %get-tuple-element.17), channel_id=1, source_target_pairs={{1,0},{2,1},{3,2},{4,3},{5,4},{6,5},{7,6},{8,7},{9,8},{10,9},{11,1... | collective-permute-start | bytes 98312 | tf_op jit(solution)/shard_map/ppermute | solution.py:20
  6.9 5.1 %copy-start = (f32[4,8,8,256]{3,2,1,0:T(8,128)S(1)}, f32[4,8,8,256]{3,2,1,0:T(8,128)}, u32[]{:S(2)}) copy-start(f32[4,8,8,256]{3,2,1,0:T(8,128)} %param.6) | copy-start | bytes 786436
  6.9 9.9 %collective-permute-start.1 = (f32[4,1,8,256]{3,2,1,0:T(8,128)S(1)}, f32[4,1,8,256]{3,2,1,0:T(8,128)S(1)}, u32[]{:S(2)}, u32[]{:S(2)}) collective-permute-start(f32[4,1,8,256]{3,2,1,0:T(8,128)S(1)} %get-tuple-element.18), channel_id=1, source_target_pairs={{0,1},{1,2},{2,3},{3,4},{4,5},{5,6},{6,7},{7,8},{8,9},{9,10},{10,1... | collective-permute-start | bytes 98312 | tf_op jit(solution)/shard_map/ppermute | solution.py:17
  11.9 4.9 %copy-start.1 = (f32[8,8,256]{2,1,0:T(8,128)S(1)}, f32[8,8,256]{2,1,0:T(8,128)}, u32[]{:S(2)}) copy-start(f32[8,8,256]{2,1,0:T(8,128)} %param.8) | copy-start | bytes 196612
  11.9 4.9 %copy-start.2 = (f32[8,8,256]{2,1,0:T(8,128)S(1)}, f32[8,8,256]{2,1,0:T(8,128)}, u32[]{:S(2)}) copy-start(f32[8,8,256]{2,1,0:T(8,128)} %param.7) | copy-start | bytes 196612
  17.2 9.3 %collective-permute-start.2 = (f32[4,1,8,256]{3,2,1,0:T(8,128)S(1)}, f32[4,1,8,256]{3,2,1,0:T(8,128)S(1)}, u32[]{:S(2)}, u32[]{:S(2)}) collective-permute-start(f32[4,1,8,256]{3,2,1,0:T(8,128)S(1)} %get-tuple-element.11), channel_id=1, source_target_pairs={{1,0},{2,1},{3,2},{4,3},{5,4},{6,5},{7,6},{8,7},{9,8},{10,9},{11,1... | collective-permute-start | bytes 98312 | tf_op jit(solution)/shard_map/ppermute | solution.py:20
  19.5 9.7 %collective-permute-start.3 = (f32[4,1,8,256]{3,2,1,0:T(8,128)S(1)}, f32[4,1,8,256]{3,2,1,0:T(8,128)S(1)}, u32[]{:S(2)}, u32[]{:S(2)}) collective-permute-start(f32[4,1,8,256]{3,2,1,0:T(8,128)S(1)} %get-tuple-element.12), channel_id=1, source_target_pairs={{0,1},{1,2},{2,3},{3,4},{4,5},{5,6},{6,7},{7,8},{8,9},{9,10},{10,1... | collective-permute-start | bytes 98312 | tf_op jit(solution)/shard_map/ppermute | solution.py:17
  30.3 30.6 %all-to-all-start = ((f32[4,64,1,256]{3,0,2,1:T(4,128)}), f32[4,64,1,256]{3,0,2,1:T(4,128)S(1)}, u32[]{:S(2)}, u32[]{:S(2)}) async-start(f32[4,64,1,256]{3,0,2,1:T(4,128)} %bitcast), calls=%async_computation | async-start | bytes 524288 | tf_op jit(solution)/shard_map/all_to_all | solution.py:88
where the time goes:
time: 88.8 us; the launch traced here: 88.3 us
  starting transfers between devices  37 us (42%)
  waiting for transfers between devices  18.8 us (21%)
  blocking collectives  17.5 us (20%)
  local copies, waits for them, and re-layouts  6.32 us (7%)
  matrix products  6.32 us (7%)
  other arithmetic  1.42 us (2%)
  between operations  1.01 us (1%)
    all_to_all x1, starting transfers between devices, body(): lax.all_to_all(flat.reshape(members_dev, groups, regions, longitudes), 'm...  17.8 us
    all_to_all x1, blocking collectives, body(): lax.all_to_all(analysed.reshape(count, 1, regions, longitudes), 'member',...  17.5 us
    all_to_all x1, waiting for transfers between devices, body(): lax.all_to_all(flat.reshape(members_dev, groups, regions, longitudes), 'm...  11.3 us
    ppermute x2, starting transfers between devices, extended(): lax.ppermute(lax.slice_in_dim(block, block.shape[dim] - width, None, axis...  10.7 us
    ppermute x2, starting transfers between devices, extended(): lax.ppermute(lax.slice_in_dim(block, 0, width, axis=dim), axis, backward)  8.4 us
    ppermute x2, waiting for transfers between devices, extended(): lax.ppermute(lax.slice_in_dim(block, block.shape[dim] - width, None, axis...  7.45 us
  transfers between devices with their start and end apart: 5, of which 3 were waited for; matrix products, arithmetic and copies ran while one was open for 3% of the time, Pallas kernels for 0%

commit v1 on v0

v1 whole, which is shorter than its diff:
```python
import math

import jax
import jax.numpy as jnp
from jax import lax
from jax.experimental import pallas as pl
from jax.experimental.pallas import tpu as pltpu
from jax.sharding import PartitionSpec as P

MESH = pl.DeviceIdType.MESH
F32 = jnp.float32
BF16 = jnp.bfloat16
HALF_STEP = 0.15
LANES = 128


def split(x):
    high = x.astype(BF16)
    low = (x - high.astype(F32)).astype(BF16)
    return high, low


def dot(a, b):
    return lax.dot_general(a, b, (((1,), (0,)), ((), ())), preferred_element_type=F32)


def dot3(a, b):
    return dot(a[0], b[0]) + (dot(a[0], b[1]) + dot(a[1], b[0]))


def analyse(ensemble, cells, values, weights):
    count, lons = ensemble.shape
    obs = cells.shape[1]
    inflate = count - 1.0
    mean = jnp.sum(ensemble, axis=0, keepdims=True) * (1.0 / count)
    pert = ensemble - mean
    pick = jnp.where(lax.broadcasted_iota(jnp.int32, (lons, obs), 0) == cells, 1.0, 0.0).astype(BF16)
    pert_s = split(pert)
    picked = dot(pert_s[0], pick) + dot(pert_s[1], pick)
    mean_s = split(jnp.broadcast_to(mean, (8, lons)))
    obs_mean = dot(mean_s[0], pick) + dot(mean_s[1], pick)
    root_weight = jnp.sqrt(weights)
    scaled = picked * root_weight
    target = (values - obs_mean) * root_weight
    scaled_s = split(scaled)
    turned_s = (scaled_s[0].T, scaled_s[1].T)
    gram = dot3(turned_s, scaled_s)
    cross = dot3(turned_s, pert_s)
    trace = jnp.sum(jnp.sum(scaled * scaled, axis=0, keepdims=True), axis=1, keepdims=True)
    square = jnp.sum(jnp.sum(gram * gram, axis=0, keepdims=True), axis=1, keepdims=True)
    frob = jnp.sqrt(square + 2.0 * inflate * trace + inflate * inflate * count)
    unit = 1.0 / frob
    a0 = inflate * unit
    p1 = 1.5 - 0.5 * a0
    q2 = a0 * p1 * p1
    p2 = 1.5 - 0.5 * q2
    q3 = q2 * p2 * p2
    p3 = 1.5 - 0.5 * q3
    z0 = p1 * p2 * p3
    diagonal = lax.broadcasted_iota(jnp.int32, (obs, obs), 0) == lax.broadcasted_iota(jnp.int32, (obs, obs), 1)
    eye = jnp.where(diagonal, 1.0, 0.0)
    s = gram * unit
    s_s = split(s)
    s2 = dot3(s_s, s_s)
    t2 = (p1 * p1 - a0 * p1) * eye + (0.25 * a0 - p1) * s + 0.25 * s2
    m2 = dot3(s_s, split(t2))
    f2 = p2 * eye - 0.5 * m2
    e = p1 * t2 - 0.5 * m2
    f2_s = split(f2)
    u = dot3(f2_s, f2_s) - (0.5 * q2) * (f2 + p2 * eye)
    k = dot3(f2_s, split(e))
    r = -0.5 * (dot3(split(u), split(k)) + p3 * e + (p3 * p2) * eye)
    r_s = split(r)
    core_s = split(dot3(r_s, split(cross)))
    target_s = split(target)
    lead = 2.0 * z0 * dot3(target_s, s_s) + dot3(split(dot3(target_s, split(s2))), r_s)
    shift = unit * (z0 * z0 * dot3(target_s, split(cross)) + dot3(split(lead), core_s))
    gain = jnp.sqrt(inflate * unit)
    return (mean + shift[:1]) + (gain * z0) * pert + (gain * unit) * dot3(scaled_s, core_s)


def around(x, shift):
    lons = x.shape[-1]
    return pltpu.roll(x.reshape(-1, lons), shift, 1).reshape(x.shape)


def slope(x):
    return around(x, x.shape[-1] - 1) - around(x, 1)


def flow(x, zonal):
    return x - (HALF_STEP * (zonal + x)) * slope(x)


def kernel(groups, bands, state, zonal, merid, cell, value, weight, out,
           q, u, v, cells, values, weights, low_out, high_out, low_in, high_in,
           inner, outer, gathered, result, returned,
           load_sem, halo_send, halo_recv, go_send, go_recv, back_send, back_recv, own_sem):
    me = lax.axis_index("member")
    band = lax.axis_index("lat")
    members, rows, levels, lons = state.shape
    halves = lons // LANES
    index = me // 2
    odd = me % 2
    turn = index // levels
    my_row = jnp.where(odd == 0, rows // 4 + turn, turn + (turn // 2) * (rows // 2))
    my_level = index % levels

    loads = [
        pltpu.make_async_copy(state, q, load_sem.at[0]),
        pltpu.make_async_copy(zonal, u, load_sem.at[1]),
        pltpu.make_async_copy(merid, v, load_sem.at[2]),
        pltpu.make_async_copy(cell.at[my_row], cells, load_sem.at[3]),
        pltpu.make_async_copy(value.at[my_row], values, load_sem.at[4]),
        pltpu.make_async_copy(weight.at[my_row], weights, load_sem.at[5]),
    ]
    for load in loads:
        load.start()

    barrier = pltpu.get_barrier_semaphore()
    below, above = band > 0, band < bands - 1

    @pl.when(below)
    def _():
        pl.semaphore_signal(barrier, inc=1, device_id={"lat": band - 1}, device_id_type=MESH)

    @pl.when(above)
    def _():
        pl.semaphore_signal(barrier, inc=1, device_id={"lat": band + 1}, device_id_type=MESH)

    def greet(step, carry):
        pl.semaphore_signal(barrier, inc=1, device_id={"member": lax.rem(me + step, groups)}, device_id_type=MESH)
        return carry

    lax.fori_loop(1, groups, greet, 0)

    for load in loads[:3]:
        load.wait()

    wind_v = HALF_STEP * v[...]
    wind_u = u[...]

    first, last = q[:, 0], q[:, rows - 1]
    low_out[:members] = first
    low_out[members : 2 * members] = flow(first, wind_u[0]) - wind_v[0] * q[:, 1]
    low_out[2 * members] = wind_v[0]
    high_out[:members] = last
    high_out[members : 2 * members] = flow(last, wind_u[rows - 1]) + wind_v[rows - 1] * q[:, rows - 2]
    high_out[2 * members] = wind_v[rows - 1]

    pl.semaphore_wait(barrier, groups - 1 + below.astype(jnp.int32) + above.astype(jnp.int32))

    def to_low():
        return pltpu.make_async_remote_copy(
            src_ref=low_out, dst_ref=high_in, send_sem=halo_send.at[0], recv_sem=halo_recv.at[0],
            device_id={"lat": band - 1}, device_id_type=MESH)

    def to_high():
        return pltpu.make_async_remote_copy(
            src_ref=high_out, dst_ref=low_in, send_sem=halo_send.at[1], recv_sem=halo_recv.at[1],
            device_id={"lat": band + 1}, device_id_type=MESH)

    @pl.when(below)
    def _():
        to_low().start()

    @pl.when(above)
    def _():
        to_high().start()

    def advance(x, top, bottom, row, length):
        return flow(x, wind_u[row : row + length]) - wind_v[row : row + length] * (top - bottom)

    def put(block, x, place):
        for half in range(halves):
            for member in range(members):
                block[pl.ds(place * 8 + half * members + member, levels, stride=8), :] = (
                    x[member, :, half * LANES : (half + 1) * LANES])

    old = q[...]
    mid = advance(old[:, 1 : rows - 1], old[:, 2:], old[:, : rows - 2], 1, rows - 2)
    new = advance(mid[:, 1 : rows - 3], mid[:, 2:], mid[:, : rows - 4], 2, rows - 4)
    for row in range(rows - 4):
        put(inner, new[:, row], row * levels)

    def send(block, parity):
        def go(step, carry):
            place = lax.rem(index + step, groups // 2)
            peer = 2 * place + parity

            @pl.when(peer != me)
            def _():
                pltpu.make_async_remote_copy(
                    src_ref=block.at[pl.ds(pl.multiple_of(place * 8, 8), 8)],
                    dst_ref=gathered.at[pl.ds(pl.multiple_of(me * 8, 8), 8)],
                    send_sem=go_send, recv_sem=go_recv, device_id={"member": peer}, device_id_type=MESH).start()

            return carry

        lax.fori_loop(0, groups // 2, go, 0)

    def keep(block):
        return pltpu.make_async_copy(
            block.at[pl.ds(pl.multiple_of(index * 8, 8), 8)],
            gathered.at[pl.ds(pl.multiple_of(me * 8, 8), 8)], own_sem.at[0])

    send(inner, 0)

    @pl.when(below)
    def _():
        to_high().wait_recv()

    @pl.when(band == 0)
    def _():
        low_in[...] = jnp.zeros_like(low_in)

    @pl.when(above)
    def _():
        to_low().wait_recv()

    @pl.when(band == bands - 1)
    def _():
        high_in[...] = jnp.zeros_like(high_in)

    before = low_in[members : 2 * members] - low_in[2 * members] * first
    after = high_in[members : 2 * members] + high_in[2 * members] * last
    row0 = flow(first, wind_u[0]) - wind_v[0] * (old[:, 1] - low_in[:members])
    row7 = flow(last, wind_u[rows - 1]) - wind_v[rows - 1] * (high_in[:members] - old[:, rows - 2])
    put(outer, flow(row0, wind_u[0]) - wind_v[0] * (mid[:, 0] - before), 0)
    put(outer, flow(mid[:, 0], wind_u[1]) - wind_v[1] * (mid[:, 1] - row0), levels)
    put(outer, flow(mid[:, rows - 3], wind_u[rows - 2]) - wind_v[rows - 2] * (row7 - mid[:, rows - 4]), 2 * levels)
    put(outer, flow(row7, wind_u[rows - 1]) - wind_v[rows - 1] * (after - mid[:, rows - 3]), 3 * levels)
    send(outer, 1)

    @pl.when(odd == 0)
    def _():
        keep(inner).start()

    @pl.when(odd == 1)
    def _():
        keep(outer).start()

    keep(inner).wait()
    for load in loads[3:]:
        load.wait()
    others = (groups - 1) * 8
    pltpu.make_async_copy(gathered.at[pl.ds(0, others)], gathered.at[pl.ds(0, others)], go_recv).wait()

    ensemble = jnp.concatenate(
        [jnp.concatenate(
            [gathered[pl.ds(half * members + member, groups, stride=8), :] for member in range(members)], axis=0)
         for half in range(halves)], axis=1)
    analysed = analyse(
        ensemble, cells[pl.ds(my_level, 1), :], values[pl.ds(my_level, 1), :], weights[pl.ds(my_level, 1), :])
    for half in range(halves):
        for member in range(members):
            result[pl.ds(half * members + member, groups, stride=8), :] = (
                analysed[member * groups : (member + 1) * groups, half * LANES : (half + 1) * LANES])

    mine = pl.ds(pl.multiple_of(me * 8, 8), 8)

    def give(step, carry):
        peer = lax.rem(me + step, groups)
        pltpu.make_async_remote_copy(
            src_ref=result.at[pl.ds(pl.multiple_of(peer * 8, 8), 8)], dst_ref=returned.at[mine],
            send_sem=back_send, recv_sem=back_recv, device_id={"member": peer}, device_id_type=MESH).start()
        return carry

    lax.fori_loop(1, groups, give, 0)
    own = pltpu.make_async_copy(result.at[mine], returned.at[mine], own_sem.at[1])
    own.start()
    own.wait()
    pltpu.make_async_copy(returned.at[pl.ds(0, others)], returned.at[pl.ds(0, others)], back_recv).wait()

    for row in range(rows):
        parity = 0 if rows // 4 <= row < rows - rows // 4 else 1
        block = row - rows // 4 if parity == 0 else (row if row < rows // 4 else row - rows // 2)
        for half in range(halves):
            for member in range(members):
                start = (2 * block * levels + parity) * 8 + half * members + member
                out[member, row, :, half * LANES : (half + 1) * LANES] = returned[pl.ds(start, levels, stride=16), :]

    @pl.when(below)
    def _():
        to_low().wait_send()

    @pl.when(above)
    def _():
        to_high().wait_send()

    pltpu.make_async_copy(gathered.at[pl.ds(0, others)], gathered.at[pl.ds(0, others)], go_send).wait()
    pltpu.make_async_copy(returned.at[pl.ds(0, others)], returned.at[pl.ds(0, others)], back_send).wait()


def solution(mesh):
    groups, bands = mesh.shape["member"], mesh.shape["lat"]

    def body(state, zonal, merid, cell, value, weight):
        members, rows, levels, lons = state.shape
        obs = cell.shape[-1]
        halo = (2 * members + 1, levels, lons)
        tiles = groups * 8
        return pl.pallas_call(
            lambda *refs: kernel(groups, bands, *refs),
            out_shape=jax.ShapeDtypeStruct(state.shape, F32),
            in_specs=[pl.BlockSpec(memory_space=pl.ANY)] * 6,
            out_specs=pl.BlockSpec(memory_space=pltpu.VMEM),
            scratch_shapes=[
                pltpu.VMEM(state.shape, F32),
                pltpu.VMEM(zonal.shape, F32),
                pltpu.VMEM(merid.shape, F32),
                pltpu.VMEM((levels, obs), jnp.int32),
                pltpu.VMEM((levels, obs), F32),
                pltpu.VMEM((levels, obs), F32),
                pltpu.VMEM(halo, F32),
                pltpu.VMEM(halo, F32),
                pltpu.VMEM(halo, F32),
                pltpu.VMEM(halo, F32),
                pltpu.VMEM((tiles // 2, LANES), F32),
                pltpu.VMEM((tiles // 2, LANES), F32),
                pltpu.VMEM((tiles, LANES), F32),
                pltpu.VMEM((tiles, LANES), F32),
                pltpu.VMEM((tiles, LANES), F32),
                pltpu.SemaphoreType.DMA((6,)),
                pltpu.SemaphoreType.DMA((2,)),
                pltpu.SemaphoreType.DMA((2,)),
                pltpu.SemaphoreType.DMA,
                pltpu.SemaphoreType.DMA,
                pltpu.SemaphoreType.DMA,
                pltpu.SemaphoreType.DMA,
                pltpu.SemaphoreType.DMA((2,)),
            ],
            compiler_params=pltpu.CompilerParams(collective_id=0, has_side_effects=True, vmem_limit_bytes=32 * 1024 * 1024),
        )(state, zonal, merid, cell, value, weight)

    in_specs = (P("member", "lat", None, None),) + (P("lat", None, None),) * 5
    return jax.shard_map(body, mesh=mesh, in_specs=in_specs, out_specs=P("member", "lat", None, None), check_vma=False)
```

time: 88.8 us -> 48.3 us (0.54)
  the two profiles are of different devices: /device:TPU:129 before, /device:TPU:65 now
where the time goes in v1:
time: 48.3 us; the launch traced here: 47.8 us
  Pallas kernels  42.2 us (87%)
  local copies, waits for them, and re-layouts  5.6 us (12%)
    pallas_call x1, Pallas kernels, body(): pl.pallas_call(lambda *refs: kernel(groups, bands, *refs), out_shape=jax....  42.2 us
    unnamed x13, local copies, waits for them, and re-layouts  5.6 us

profile of v1, /device:TPU:65, one launch (start us, length us, event | category | flops | bytes accessed | tf_op | source)
XLA Modules:
  0.0 47.8 jit_solution(15771802699652588653)
XLA Ops:
  0.0 0.0 copy-start
  0.0 0.9 %copy-done = f32[4,8,8,256]{3,2,1,0:T(8,128)S(1)} copy-done((f32[4,8,8,256]{3,2,1,0:T(8,128)S(1)}, f32[4,8,8,256]{3,2,1,0:T(8,128)}, u32[]{:S(2)}) %copy-start) | copy-done | bytes 262168
  1.0 0.0 copy-start.1
  1.0 0.8 %copy-done.1 = f32[8,8,256]{2,1,0:T(8,128)S(1)} copy-done((f32[8,8,256]{2,1,0:T(8,128)S(1)}, f32[8,8,256]{2,1,0:T(8,128)}, u32[]{:S(2)}) %copy-start.1) | copy-done | bytes 65560
  1.8 0.0 copy-start.2
  1.8 0.8 %copy-done.2 = f32[8,8,256]{2,1,0:T(8,128)S(1)} copy-done((f32[8,8,256]{2,1,0:T(8,128)S(1)}, f32[8,8,256]{2,1,0:T(8,128)}, u32[]{:S(2)}) %copy-start.2) | copy-done | bytes 65560
  2.6 0.0 copy-start.3
  2.6 0.8 %copy-done.3 = s32[8,8,128]{2,1,0:T(8,128)S(1)} copy-done((s32[8,8,128]{2,1,0:T(8,128)S(1)}, s32[8,8,128]{2,1,0:T(8,128)}, u32[]{:S(2)}) %copy-start.3) | copy-done | bytes 32792
  3.4 0.0 copy-start.4
  3.4 0.8 %copy-done.4 = f32[8,8,128]{2,1,0:T(8,128)S(1)} copy-done((f32[8,8,128]{2,1,0:T(8,128)S(1)}, f32[8,8,128]{2,1,0:T(8,128)}, u32[]{:S(2)}) %copy-start.4) | copy-done | bytes 32792
  4.1 0.0 copy-start.5
  4.2 0.8 %copy-done.5 = f32[8,8,128]{2,1,0:T(8,128)S(1)} copy-done((f32[8,8,128]{2,1,0:T(8,128)S(1)}, f32[8,8,128]{2,1,0:T(8,128)}, u32[]{:S(2)}) %copy-start.5) | copy-done | bytes 32792
  4.9 42.2 %shard_map.64 = f32[4,8,8,256]{3,2,1,0:T(8,128)S(1)} custom-call(f32[4,8,8,256]{3,2,1,0:T(8,128)S(1)} %copy-done, f32[8,8,256]{2,1,0:T(8,128)S(1)} %copy-done.1, f32[8,8,256]{2,1,0:T(8,128)S(1)} %copy-done.2, s32[8,8,128]{2,1,0:T(8,128)S(1)} %copy-done.3, f32[8,8,128]{2,1,0:T(8,128)S(1)} %copy-done.4, f32[8,8,128]{2,1,0:T(8,128)S(1)} %copy-done.5), custom_call_target="tpu_custom_call" | custom-call | tf_op jit(solution)/shard_map/pallas_call | solution.py:303
  47.1 0.7 %copy.8 = f32[4,8,8,256]{3,2,1,0:T(8,128)} copy(f32[4,8,8,256]{3,2,1,0:T(8,128)S(1)} %shard_map.64) | data formatting | bytes 524288
Async XLA Ops:
  0.0 0.9 %copy-start = (f32[4,8,8,256]{3,2,1,0:T(8,128)S(1)}, f32[4,8,8,256]{3,2,1,0:T(8,128)}, u32[]{:S(2)}) copy-start(f32[4,8,8,256]{3,2,1,0:T(8,128)} %refs_0_.1) | copy-start | bytes 786436
  1.0 0.8 %copy-start.1 = (f32[8,8,256]{2,1,0:T(8,128)S(1)}, f32[8,8,256]{2,1,0:T(8,128)}, u32[]{:S(2)}) copy-start(f32[8,8,256]{2,1,0:T(8,128)} %refs_1_.1) | copy-start | bytes 196612
  1.8 0.8 %copy-start.2 = (f32[8,8,256]{2,1,0:T(8,128)S(1)}, f32[8,8,256]{2,1,0:T(8,128)}, u32[]{:S(2)}) copy-start(f32[8,8,256]{2,1,0:T(8,128)} %refs_2_.1) | copy-start | bytes 196612
  2.6 0.8 %copy-start.3 = (s32[8,8,128]{2,1,0:T(8,128)S(1)}, s32[8,8,128]{2,1,0:T(8,128)}, u32[]{:S(2)}) copy-start(s32[8,8,128]{2,1,0:T(8,128)} %refs_3_.1) | copy-start | bytes 98308
  3.4 0.8 %copy-start.4 = (f32[8,8,128]{2,1,0:T(8,128)S(1)}, f32[8,8,128]{2,1,0:T(8,128)}, u32[]{:S(2)}) copy-start(f32[8,8,128]{2,1,0:T(8,128)} %refs_4_.1) | copy-start | bytes 98308
  4.1 0.8 %copy-start.5 = (f32[8,8,128]{2,1,0:T(8,128)S(1)}, f32[8,8,128]{2,1,0:T(8,128)}, u32[]{:S(2)}) copy-start(f32[8,8,128]{2,1,0:T(8,128)} %refs_5_.1) | copy-start | bytes 98308

commit v2 on v1

--- a/solution.py
+++ b/solution.py
@@ -95,7 +95,7 @@
 def kernel(groups, bands, state, zonal, merid, cell, value, weight, out,
            q, u, v, cells, values, weights, low_out, high_out, low_in, high_in,
            inner, outer, gathered, result, returned,
-           load_sem, halo_send, halo_recv, go_send, go_recv, back_send, back_recv, own_sem):
+           load_sem, halo_send, halo_recv, go_send, go_recv, back_send, back_recv, own_sem, ready, band_ready):
     me = lax.axis_index("member")
     band = lax.axis_index("lat")
     members, rows, levels, lons = state.shape
@@ -119,17 +119,20 @@
 
     barrier = pltpu.get_barrier_semaphore()
     below, above = band > 0, band < bands - 1
+    peers_x, peers_y = groups // 8, 4
+    my_x, my_y = index // peers_y, index % peers_y
 
     @pl.when(below)
     def _():
         pl.semaphore_signal(barrier, inc=1, device_id={"lat": band - 1}, device_id_type=MESH)
 
-    @pl.when(above)
-    def _():
-        pl.semaphore_signal(barrier, inc=1, device_id={"lat": band + 1}, device_id_type=MESH)
-
     def greet(step, carry):
-        pl.semaphore_signal(barrier, inc=1, device_id={"member": lax.rem(me + step, groups)}, device_id_type=MESH)
+        peer = lax.rem(me + step, groups)
+
+        @pl.when(me > 0)
+        def _():
+            pl.semaphore_signal(barrier, inc=1, device_id={"member": peer}, device_id_type=MESH)
+
         return carry
 
     lax.fori_loop(1, groups, greet, 0)
@@ -148,7 +151,20 @@
     high_out[members : 2 * members] = flow(last, wind_u[rows - 1]) + wind_v[rows - 1] * q[:, rows - 2]
     high_out[2 * members] = wind_v[rows - 1]
 
-    pl.semaphore_wait(barrier, groups - 1 + below.astype(jnp.int32) + above.astype(jnp.int32))
+    pl.semaphore_wait(barrier, groups - 2 + (me == 0).astype(jnp.int32) + above.astype(jnp.int32))
+
+    @pl.when(above)
+    def _():
+        pl.semaphore_signal(band_ready, inc=1, device_id={"lat": band + 1}, device_id_type=MESH)
+
+    @pl.when(me == 0)
+    def _():
+        def answer(step, carry):
+            pl.semaphore_signal(ready, inc=1, device_id={"member": step}, device_id_type=MESH)
+            return carry
+
+        lax.fori_loop(1, groups, answer, 0)
+
 
     def to_low():
         return pltpu.make_async_remote_copy(
@@ -159,10 +175,6 @@
         return pltpu.make_async_remote_copy(
             src_ref=high_out, dst_ref=low_in, send_sem=halo_send.at[1], recv_sem=halo_recv.at[1],
             device_id={"lat": band + 1}, device_id_type=MESH)
-
-    @pl.when(below)
-    def _():
-        to_low().start()
 
     @pl.when(above)
     def _():
@@ -183,21 +195,29 @@
     for row in range(rows - 4):
         put(inner, new[:, row], row * levels)
 
+    def place_of(step):
+        turn = step // peers_y
+        far = peers_x // 2 + ((turn + 1) // 2) * (2 * (turn % 2) - 1)
+        return lax.rem(my_x + far, peers_x) * peers_y + lax.rem(my_y + 1 + step, peers_y)
+
+    def go(block, place, parity):
+        return pltpu.make_async_remote_copy(
+            src_ref=block.at[pl.ds(pl.multiple_of(place * 8, 8), 8)],
+            dst_ref=gathered.at[pl.ds(pl.multiple_of(me * 8, 8), 8)],
+            send_sem=go_send, recv_sem=go_recv, device_id={"member": 2 * place + parity}, device_id_type=MESH)
+
     def send(block, parity):
-        def go(step, carry):
-            place = lax.rem(index + step, groups // 2)
+        def start(step, carry):
+            place = place_of(step)
             peer = 2 * place + parity
 
-            @pl.when(peer != me)
+            @pl.when((peer != me) & (peer > 0))
             def _():
-                pltpu.make_async_remote_copy(
-                    src_ref=block.at[pl.ds(pl.multiple_of(place * 8, 8), 8)],
-                    dst_ref=gathered.at[pl.ds(pl.multiple_of(me * 8, 8), 8)],
-                    send_sem=go_send, recv_sem=go_recv, device_id={"member": peer}, device_id_type=MESH).start()
+                go(block, place, parity).start()
 
             return carry
 
-        lax.fori_loop(0, groups // 2, go, 0)
+        lax.fori_loop(0, groups // 2, start, 0)
 
     def keep(block):
         return pltpu.make_async_copy(
@@ -205,6 +225,11 @@
             gathered.at[pl.ds(pl.multiple_of(me * 8, 8), 8)], own_sem.at[0])
 
     send(inner, 0)
+
+    @pl.when(below)
+    def _():
+        pl.semaphore_wait(band_ready, 1)
+        to_low().start()
 
     @pl.when(below)
     def _():
@@ -231,6 +256,11 @@
     put(outer, flow(mid[:, rows - 3], wind_u[rows - 2]) - wind_v[rows - 2] * (row7 - mid[:, rows - 4]), 2 * levels)
     put(outer, flow(row7, wind_u[rows - 1]) - wind_v[rows - 1] * (after - mid[:, rows - 3]), 3 * levels)
     send(outer, 1)
+
+    @pl.when(me > 0)
+    def _():
+        pl.semaphore_wait(ready, 1)
+        go(inner, 0, 0).start()
 
     @pl.when(odd == 0)
     def _():
@@ -260,13 +290,17 @@
     mine = pl.ds(pl.multiple_of(me * 8, 8), 8)
 
     def give(step, carry):
-        peer = lax.rem(me + step, groups)
-        pltpu.make_async_remote_copy(
-            src_ref=result.at[pl.ds(pl.multiple_of(peer * 8, 8), 8)], dst_ref=returned.at[mine],
-            send_sem=back_send, recv_sem=back_recv, device_id={"member": peer}, device_id_type=MESH).start()
+        peer = 2 * place_of(step // 2) + lax.rem(me + 1 + step, 2)
+
+        @pl.when(peer != me)
+        def _():
+            pltpu.make_async_remote_copy(
+                src_ref=result.at[pl.ds(pl.multiple_of(peer * 8, 8), 8)], dst_ref=returned.at[mine],
+                send_sem=back_send, recv_sem=back_recv, device_id={"member": peer}, device_id_type=MESH).start()
+
         return carry
 
-    lax.fori_loop(1, groups, give, 0)
+    lax.fori_loop(0, groups, give, 0)
     own = pltpu.make_async_copy(result.at[mine], returned.at[mine], own_sem.at[1])
     own.start()
     own.wait()
@@ -329,8 +363,10 @@
                 pltpu.SemaphoreType.DMA,
                 pltpu.SemaphoreType.DMA,
                 pltpu.SemaphoreType.DMA((2,)),
+                pltpu.SemaphoreType.REGULAR,
+                pltpu.SemaphoreType.REGULAR,
             ],
-            compiler_params=pltpu.CompilerParams(collective_id=0, has_side_effects=True, vmem_limit_bytes=32 * 1024 * 1024),
+            compiler_params=pltpu.CompilerParams(collective_id=0, has_side_effects=True, vmem_limit_bytes=60 * 1024 * 1024),
         )(state, zonal, merid, cell, value, weight)
 
     in_specs = (P("member", "lat", None, None),) + (P("lat", None, None),) * 5

time: 48.3 us -> 44.5 us (0.921)
  the two profiles are of different devices: /device:TPU:65 before, /device:TPU:897 now
where the time goes in v2:
time: 44.5 us; the launch traced here: 44.3 us
  Pallas kernels  42.6 us (96%)
  local copies, waits for them, and re-layouts  1.67 us (4%)
    pallas_call x1, Pallas kernels, body(): pl.pallas_call(lambda *refs: kernel(groups, bands, *refs), out_shape=jax....  42.6 us
    unnamed x1, local copies, waits for them, and re-layouts  1.67 us

profile of v2, /device:TPU:897, one launch (start us, length us, event | category | flops | bytes accessed | tf_op | source)
XLA Modules:
  0.0 44.3 jit_solution(8804874512674977058)
XLA Ops:
  0.0 42.6 %shard_map.64 = f32[4,8,8,256]{3,2,1,0:T(8,128)} custom-call(f32[4,8,8,256]{3,2,1,0:T(8,128)} %refs_0_.1, f32[8,8,256]{2,1,0:T(8,128)} %refs_1_.1, f32[8,8,256]{2,1,0:T(8,128)} %refs_2_.1, s32[8,8,128]{2,1,0:T(8,128)} %refs_3_.1, f32[8,8,128]{2,1,0:T(8,128)} %refs_4_.1, f32[8,8,128]{2,1,0:T(8,128)} %refs_5_.1), custom_call_target="tpu_custom_call" | custom-call | tf_op jit(solution)/shard_map/pallas_call | solution.py:337
  42.6 1.7 %copy.8 = f32[4,8,8,256]{3,2,1,0:T(8,128)} copy(f32[4,8,8,256]{3,2,1,0:T(8,128)} %shard_map.64) | data formatting | bytes 524288

commit v3 on v2

v3 whole, which is shorter than its diff:
```python
import math

import jax
import jax.numpy as jnp
from jax import lax
from jax.experimental import pallas as pl
from jax.experimental.pallas import tpu as pltpu
from jax.sharding import PartitionSpec as P

MESH = pl.DeviceIdType.MESH
F32 = jnp.float32
BF16 = jnp.bfloat16
HALF_STEP = 0.15
LANES = 128
SIDE_X, SIDE_Y = 8, 4
FAR_X = (4, 5, 3, 6, 2, 7, 1, 0)
FAR_Y = (2, 1, 3, 0)


def split(x):
    high = x.astype(BF16)
    low = (x - high.astype(F32)).astype(BF16)
    return high, low


def dot(a, b):
    return lax.dot_general(a, b, (((1,), (0,)), ((), ())), preferred_element_type=F32)


def dot3(a, b):
    return dot(a[0], b[0]) + (dot(a[0], b[1]) + dot(a[1], b[0]))


def analyse(ensemble, cells, values, weights):
    count, lons = ensemble.shape
    obs = cells.shape[1]
    inflate = count - 1.0
    mean = jnp.sum(ensemble, axis=0, keepdims=True) * (1.0 / count)
    pert = ensemble - mean
    pick = jnp.where(lax.broadcasted_iota(jnp.int32, (lons, obs), 0) == cells, 1.0, 0.0).astype(BF16)
    pert_s = split(pert)
    picked = dot(pert_s[0], pick) + dot(pert_s[1], pick)
    mean_s = split(jnp.broadcast_to(mean, (8, lons)))
    obs_mean = dot(mean_s[0], pick) + dot(mean_s[1], pick)
    root_weight = jnp.sqrt(weights)
    scaled = picked * root_weight
    target = (values - obs_mean) * root_weight
    scaled_s = split(scaled)
    turned_s = (scaled_s[0].T, scaled_s[1].T)
    gram = dot3(turned_s, scaled_s)
    cross = dot3(turned_s, pert_s)
    trace = jnp.sum(jnp.sum(scaled * scaled, axis=0, keepdims=True), axis=1, keepdims=True)
    square = jnp.sum(jnp.sum(gram * gram, axis=0, keepdims=True), axis=1, keepdims=True)
    frob = jnp.sqrt(square + 2.0 * inflate * trace + inflate * inflate * count)
    unit = 1.0 / frob
    a0 = inflate * unit
    p1 = 1.5 - 0.5 * a0
    q2 = a0 * p1 * p1
    p2 = 1.5 - 0.5 * q2
    q3 = q2 * p2 * p2
    p3 = 1.5 - 0.5 * q3
    z0 = p1 * p2 * p3
    diagonal = lax.broadcasted_iota(jnp.int32, (obs, obs), 0) == lax.broadcasted_iota(jnp.int32, (obs, obs), 1)
    eye = jnp.where(diagonal, 1.0, 0.0)
    s = gram * unit
    s_s = split(s)
    s2 = dot3(s_s, s_s)
    t2 = (p1 * p1 - a0 * p1) * eye + (0.25 * a0 - p1) * s + 0.25 * s2
    m2 = dot3(s_s, split(t2))
    f2 = p2 * eye - 0.5 * m2
    e = p1 * t2 - 0.5 * m2
    f2_s = split(f2)
    u = dot3(f2_s, f2_s) - (0.5 * q2) * (f2 + p2 * eye)
    k = dot3(f2_s, split(e))
    r = -0.5 * (dot3(split(u), split(k)) + p3 * e + (p3 * p2) * eye)
    r_s = split(r)
    core_s = split(dot3(r_s, split(cross)))
    target_s = split(target)
    lead = 2.0 * z0 * dot3(target_s, s_s) + dot3(split(dot3(target_s, split(s2))), r_s)
    shift = unit * (z0 * z0 * dot3(target_s, split(cross)) + dot3(split(lead), core_s))
    gain = jnp.sqrt(inflate * unit)
    return (mean + shift[:1]) + (gain * z0) * pert + (gain * unit) * dot3(scaled_s, core_s)


def around(x, shift):
    lons = x.shape[-1]
    return pltpu.roll(x.reshape(-1, lons), shift, 1).reshape(x.shape)


def slope(x):
    return around(x, x.shape[-1] - 1) - around(x, 1)


def flow(x, zonal):
    return x - (HALF_STEP * (zonal + x)) * slope(x)


def kernel(groups, bands, state, zonal, merid, cell, value, weight, out,
           q, u, v, cells, values, weights, low_in, high_in, low_next, high_next, low_out, high_out,
           inner, outer, edge, gathered, result, returned,
           load_sem, halo_send, halo_recv, go_send, go_recv, back_send, back_recv, own_sem, ready, band_ready):
    me = lax.axis_index("member")
    band = lax.axis_index("lat")
    members, rows, levels, lons = state.shape
    halves = lons // LANES
    index, odd = me // 2, me % 2
    my_x, my_y = index // SIDE_Y, index % SIDE_Y
    my_row = jnp.where(odd == 0, 2 + my_y, my_y + 1 - 2 * (my_y % 2) + 4 * (my_y // 2))
    my_level = my_x
    below, above = band > 0, band < bands - 1

    loads = [
        pltpu.make_async_copy(state, q, load_sem.at[0]),
        pltpu.make_async_copy(zonal, u, load_sem.at[1]),
        pltpu.make_async_copy(merid, v, load_sem.at[2]),
        pltpu.make_async_copy(cell.at[my_row], cells, load_sem.at[3]),
        pltpu.make_async_copy(value.at[my_row], values, load_sem.at[4]),
        pltpu.make_async_copy(weight.at[my_row], weights, load_sem.at[5]),
    ]
    for load in loads:
        load.start()

    barrier = pltpu.get_barrier_semaphore()

    @pl.when(below)
    def _():
        pl.semaphore_signal(barrier, inc=1, device_id={"lat": band - 1}, device_id_type=MESH)

    @pl.when(me > 0)
    def _():
        def greet(step, carry):
            pl.semaphore_signal(barrier, inc=1, device_id={"member": lax.rem(me + step, groups)}, device_id_type=MESH)
            return carry

        lax.fori_loop(1, groups, greet, 0)

    pl.semaphore_wait(barrier, groups - 2 + (me == 0).astype(jnp.int32) + above.astype(jnp.int32))

    def to_band(number, src, dst, step):
        return pltpu.make_async_remote_copy(
            src_ref=src, dst_ref=dst, send_sem=halo_send.at[number], recv_sem=halo_recv.at[number],
            device_id={"lat": band + step}, device_id_type=MESH)

    def row_up():
        return to_band(0, state.at[:, rows - 1], low_in, 1)

    def row_down():
        return to_band(1, state.at[:, 0], high_in, -1)

    def next_up():
        return to_band(2, high_out, low_next, 1)

    def next_down():
        return to_band(3, low_out, high_next, -1)

    @pl.when(above)
    def _():
        pl.semaphore_signal(band_ready, inc=1, device_id={"lat": band + 1}, device_id_type=MESH)
        row_up().start()

    @pl.when(me == 0)
    def _():
        def answer(step, carry):
            pl.semaphore_signal(ready, inc=1, device_id={"member": step}, device_id_type=MESH)
            return carry

        lax.fori_loop(1, groups, answer, 0)

    @pl.when(below & (me > 0))
    def _():
        pl.semaphore_wait(band_ready, 1)
        row_down().start()

    for load in loads[:3]:
        load.wait()

    wind_u, wind_v = u[...], HALF_STEP * v[...]

    def put(block, x, place, every):
        for half in range(halves):
            for member in range(members):
                block[pl.ds(place * 8 + half * members + member, levels, stride=8 * every), :] = (
                    x[member, :, half * LANES : (half + 1) * LANES])

    old = q[...]
    mid = flow(old[:, 1:7], wind_u[1:7]) - wind_v[1:7] * (old[:, 2:] - old[:, :6])
    new = flow(mid[:, 1:5], wind_u[2:6]) - wind_v[2:6] * (mid[:, 2:] - mid[:, :4])
    for row in range(4):
        put(inner, new[:, row], row, 4)

    far_x = [(lax.rem(my_x + dx, SIDE_X)) for dx in FAR_X]
    far_y = [(lax.rem(my_y + dy, SIDE_Y)) for dy in FAR_Y]
    mine = pl.ds(pl.multiple_of(me * 8, 8), 8)

    def go(block, tile, peer):
        return pltpu.make_async_remote_copy(
            src_ref=block.at[pl.ds(pl.multiple_of(tile * 8, 8), 8)], dst_ref=gathered.at[mine],
            send_sem=go_send, recv_sem=go_recv, device_id={"member": peer}, device_id_type=MESH)

    for x in far_x:
        for y in far_y:
            tile = x * SIDE_Y + y

            @pl.when((tile > 0) & (2 * tile != me))
            def _():
                go(inner, tile, 2 * tile).start()

    @pl.when(below & (me == 0))
    def _():
        pl.semaphore_wait(band_ready, 1)
        row_down().start()

    first, last = old[:, 0], old[:, 7]

    @pl.when(below)
    def _():
        row_up().wait_recv()

    @pl.when(band == 0)
    def _():
        low_in[...] = jnp.zeros_like(low_in)
        low_next[...] = jnp.zeros_like(low_next)

    row0 = flow(first, wind_u[0]) - wind_v[0] * (old[:, 1] - low_in[...])
    low_out[...] = row0

    @pl.when(below)
    def _():
        next_down().start()

    @pl.when(above)
    def _():
        row_down().wait_recv()

    @pl.when(band == bands - 1)
    def _():
        high_in[...] = jnp.zeros_like(high_in)
        high_next[...] = jnp.zeros_like(high_next)

    row7 = flow(last, wind_u[7]) - wind_v[7] * (high_in[...] - old[:, 6])
    high_out[...] = row7

    @pl.when(above)
    def _():
        next_up().start()

    put(outer, flow(mid[:, 0], wind_u[1]) - wind_v[1] * (mid[:, 1] - row0), 0, 2)
    put(outer, flow(mid[:, 5], wind_u[6]) - wind_v[6] * (row7 - mid[:, 4]), 1, 2)

    def send_odd(block, near, far):
        for x in far_x:
            for slot, y in enumerate((near, far)):
                peer = x * 8 + 2 * y + 1

                @pl.when(peer != me)
                def _():
                    go(block, x * 2 + slot, peer).start()

    send_odd(outer, 0, 3)

    @pl.when(below)
    def _():
        next_up().wait_recv()

    @pl.when(above)
    def _():
        next_down().wait_recv()

    put(edge, flow(row0, wind_u[0]) - wind_v[0] * (mid[:, 0] - low_next[...]), 0, 2)
    put(edge, flow(row7, wind_u[7]) - wind_v[7] * (high_next[...] - mid[:, 5]), 1, 2)
    send_odd(edge, 1, 2)

    def keep(block, tile):
        return pltpu.make_async_copy(block.at[pl.ds(pl.multiple_of(tile * 8, 8), 8)], gathered.at[mine], own_sem.at[0])

    @pl.when(odd == 0)
    def _():
        keep(inner, index).start()

    @pl.when((odd == 1) & ((my_y == 0) | (my_y == 3)))
    def _():
        keep(outer, my_x * 2 + my_y // 3).start()

    @pl.when((odd == 1) & ((my_y == 1) | (my_y == 2)))
    def _():
        keep(edge, my_x * 2 + my_y // 2).start()

    @pl.when(me > 0)
    def _():
        pl.semaphore_wait(ready, 1)
        go(inner, 0, 0).start()

    keep(inner, index).wait()
    for load in loads[3:]:
        load.wait()
    others = pl.ds(0, (groups - 1) * 8)
    pltpu.make_async_copy(gathered.at[others], gathered.at[others], go_recv).wait()

    ensemble = jnp.concatenate(
        [jnp.concatenate(
            [gathered[pl.ds(half * members + member, groups, stride=8), :] for member in range(members)], axis=0)
         for half in range(halves)], axis=1)
    analysed = analyse(
        ensemble, cells[pl.ds(my_level, 1), :], values[pl.ds(my_level, 1), :], weights[pl.ds(my_level, 1), :])
    for half in range(halves):
        for member in range(members):
            result[pl.ds(half * members + member, groups, stride=8), :] = (
                analysed[member * groups : (member + 1) * groups, half * LANES : (half + 1) * LANES])

    def give(peer):
        return pltpu.make_async_remote_copy(
            src_ref=result.at[pl.ds(pl.multiple_of(peer * 8, 8), 8)], dst_ref=returned.at[mine],
            send_sem=back_send, recv_sem=back_recv, device_id={"member": peer}, device_id_type=MESH)

    for x in far_x:
        for y in far_y:
            for core in range(2):
                peer = x * 8 + 2 * y + core
                if (x is far_x[-1]) and (y is far_y[-1]):

                    @pl.when(odd != core)
                    def _():
                        give(peer).start()
                else:
                    give(peer).start()

    own = pltpu.make_async_copy(result.at[mine], returned.at[mine], own_sem.at[1])
    own.start()
    own.wait()
    pltpu.make_async_copy(returned.at[others], returned.at[others], back_recv).wait()

    for row, place, core in ((2, 0, 0), (3, 1, 0), (4, 2, 0), (5, 3, 0), (1, 0, 1), (0, 1, 1), (7, 2, 1), (6, 3, 1)):
        for half in range(halves):
            for member in range(members):
                start = (2 * place + core) * 8 + half * members + member
                out[member, row, :, half * LANES : (half + 1) * LANES] = returned[pl.ds(start, levels, stride=64), :]

    @pl.when(below)
    def _():
        row_down().wait_send()
        next_down().wait_send()

    @pl.when(above)
    def _():
        row_up().wait_send()
        next_up().wait_send()

    pltpu.make_async_copy(gathered.at[others], gathered.at[others], go_send).wait()
    pltpu.make_async_copy(returned.at[others], returned.at[others], back_send).wait()


def solution(mesh):
    groups, bands = mesh.shape["member"], mesh.shape["lat"]
    assert groups == 2 * SIDE_X * SIDE_Y

    def body(state, zonal, merid, cell, value, weight):
        members, rows, levels, lons = state.shape
        obs = cell.shape[-1]
        halo = pltpu.VMEM((members, levels, lons), F32)
        tiles = groups * 8
        return pl.pallas_call(
            lambda *refs: kernel(groups, bands, *refs),
            out_shape=pltpu.VMEM(state.shape, F32),
            in_specs=[pl.BlockSpec(memory_space=pltpu.HBM)] * 6,
            out_specs=pl.BlockSpec(memory_space=pltpu.VMEM),
            scratch_shapes=[
                pltpu.VMEM(state.shape, F32),
                pltpu.VMEM(zonal.shape, F32),
                pltpu.VMEM(merid.shape, F32),
                pltpu.VMEM((levels, obs), jnp.int32),
                pltpu.VMEM((levels, obs), F32),
                pltpu.VMEM((levels, obs), F32),
                halo, halo, halo, halo, halo, halo,
                pltpu.VMEM((tiles // 2, LANES), F32),
                pltpu.VMEM((tiles // 4, LANES), F32),
                pltpu.VMEM((tiles // 4, LANES), F32),
                pltpu.VMEM((tiles, LANES), F32),
                pltpu.VMEM((tiles, LANES), F32),
                pltpu.VMEM((tiles, LANES), F32),
                pltpu.SemaphoreType.DMA((6,)),
                pltpu.SemaphoreType.DMA((4,)),
                pltpu.SemaphoreType.DMA((4,)),
                pltpu.SemaphoreType.DMA,
                pltpu.SemaphoreType.DMA,
                pltpu.SemaphoreType.DMA,
                pltpu.SemaphoreType.DMA,
                pltpu.SemaphoreType.DMA((2,)),
                pltpu.SemaphoreType.REGULAR,
                pltpu.SemaphoreType.REGULAR,
            ],
            compiler_params=pltpu.CompilerParams(collective_id=0, has_side_effects=True, vmem_limit_bytes=56 * 1024 * 1024),
        )(state, zonal, merid, cell, value, weight)

    in_specs = (P("member", "lat", None, None),) + (P("lat", None, None),) * 5
    return jax.shard_map(body, mesh=mesh, in_specs=in_specs, out_specs=P("member", "lat", None, None), check_vma=False)
```

time: 44.5 us -> 44.2 us (level)
  the two profiles are of different devices: /device:TPU:897 before, /device:TPU:769 now
where the time goes in v3:
time: 44.2 us; the launch traced here: 44.1 us
  Pallas kernels  43.3 us (98%)
  local copies, waits for them, and re-layouts  0.71 us (2%)
    pallas_call x1, Pallas kernels, body(): pl.pallas_call(lambda *refs: kernel(groups, bands, *refs), out_shape=pltp...  43.3 us

profile of v3, /device:TPU:769, one launch (start us, length us, event | category | flops | bytes accessed | tf_op | source)
XLA Modules:
  0.0 44.1 jit_solution(2600928951873608985)
XLA Ops:
  0.0 43.3 %shard_map.64 = f32[4,8,8,256]{3,2,1,0:T(8,128)S(1)} custom-call(f32[4,8,8,256]{3,2,1,0:T(8,128)} %refs_0_.1, f32[8,8,256]{2,1,0:T(8,128)} %refs_1_.1, f32[8,8,256]{2,1,0:T(8,128)} %refs_2_.1, s32[8,8,128]{2,1,0:T(8,128)} %refs_3_.1, f32[8,8,128]{2,1,0:T(8,128)} %refs_4_.1, f32[8,8,128]{2,1,0:T(8,128)} %refs_5_.1), custom_call_target="tpu_custom_call" | custom-call | tf_op jit(solution)/shard_map/pallas_call | solution.py:361
  43.4 0.7 %copy.8 = f32[4,8,8,256]{3,2,1,0:T(8,128)} copy(f32[4,8,8,256]{3,2,1,0:T(8,128)S(1)} %shard_map.64) | data formatting | bytes 524288

commit v4 on v3

--- a/solution.py
+++ b/solution.py
@@ -96,7 +96,7 @@
 
 
 def kernel(groups, bands, state, zonal, merid, cell, value, weight, out,
-           q, u, v, cells, values, weights, low_in, high_in, low_next, high_next, low_out, high_out,
+           q, u, v, cells, values, weights, low_in, high_in, low_out, high_out,
            inner, outer, edge, gathered, result, returned,
            load_sem, halo_send, halo_recv, go_send, go_recv, back_send, back_recv, own_sem, ready, band_ready):
     me = lax.axis_index("member")
@@ -105,7 +105,7 @@
     halves = lons // LANES
     index, odd = me // 2, me % 2
     my_x, my_y = index // SIDE_Y, index % SIDE_Y
-    my_row = jnp.where(odd == 0, 2 + my_y, my_y + 1 - 2 * (my_y % 2) + 4 * (my_y // 2))
+    my_row = jnp.where(odd == 0, 2 + my_y, my_y + 4 * (my_y // 2))
     my_level = my_x
     below, above = band > 0, band < bands - 1
 
@@ -120,13 +120,18 @@
     for load in loads:
         load.start()
 
+    late = (me == 0) & (band == 0)
     barrier = pltpu.get_barrier_semaphore()
 
     @pl.when(below)
     def _():
         pl.semaphore_signal(barrier, inc=1, device_id={"lat": band - 1}, device_id_type=MESH)
 
-    @pl.when(me > 0)
+    @pl.when(above & jnp.logical_not(late))
+    def _():
+        pl.semaphore_signal(barrier, inc=1, device_id={"lat": band + 1}, device_id_type=MESH)
+
+    @pl.when(jnp.logical_not(late))
     def _():
         def greet(step, carry):
             pl.semaphore_signal(barrier, inc=1, device_id={"member": lax.rem(me + step, groups)}, device_id_type=MESH)
@@ -134,47 +139,29 @@
 
         lax.fori_loop(1, groups, greet, 0)
 
-    pl.semaphore_wait(barrier, groups - 2 + (me == 0).astype(jnp.int32) + above.astype(jnp.int32))
-
-    def to_band(number, src, dst, step):
-        return pltpu.make_async_remote_copy(
-            src_ref=src, dst_ref=dst, send_sem=halo_send.at[number], recv_sem=halo_recv.at[number],
-            device_id={"lat": band + step}, device_id_type=MESH)
-
-    def row_up():
-        return to_band(0, state.at[:, rows - 1], low_in, 1)
-
-    def row_down():
-        return to_band(1, state.at[:, 0], high_in, -1)
-
-    def next_up():
-        return to_band(2, high_out, low_next, 1)
-
-    def next_down():
-        return to_band(3, low_out, high_next, -1)
-
-    @pl.when(above)
-    def _():
-        pl.semaphore_signal(band_ready, inc=1, device_id={"lat": band + 1}, device_id_type=MESH)
-        row_up().start()
-
-    @pl.when(me == 0)
-    def _():
-        def answer(step, carry):
-            pl.semaphore_signal(ready, inc=1, device_id={"member": step}, device_id_type=MESH)
-            return carry
-
-        lax.fori_loop(1, groups, answer, 0)
-
-    @pl.when(below & (me > 0))
-    def _():
-        pl.semaphore_wait(band_ready, 1)
-        row_down().start()
-
     for load in loads[:3]:
         load.wait()
 
     wind_u, wind_v = u[...], HALF_STEP * v[...]
+    old = q[...]
+    first, last = old[:, 0], old[:, 7]
+
+    low_out[:members] = first
+    low_out[members : 2 * members] = flow(first, wind_u[0]) - wind_v[0] * old[:, 1]
+    low_out[2 * members] = wind_v[0]
+    high_out[:members] = last
+    high_out[members : 2 * members] = flow(last, wind_u[7]) + wind_v[7] * old[:, 6]
+    high_out[2 * members] = wind_v[7]
+
+    def to_low():
+        return pltpu.make_async_remote_copy(
+            src_ref=low_out, dst_ref=high_in, send_sem=halo_send.at[0], recv_sem=halo_recv.at[0],
+            device_id={"lat": band - 1}, device_id_type=MESH)
+
+    def to_high():
+        return pltpu.make_async_remote_copy(
+            src_ref=high_out, dst_ref=low_in, send_sem=halo_send.at[1], recv_sem=halo_recv.at[1],
+            device_id={"lat": band + 1}, device_id_type=MESH)
 
     def put(block, x, place, every):
         for half in range(halves):
@@ -182,12 +169,34 @@
                 block[pl.ds(place * 8 + half * members + member, levels, stride=8 * every), :] = (
                     x[member, :, half * LANES : (half + 1) * LANES])
 
-    old = q[...]
     mid = flow(old[:, 1:7], wind_u[1:7]) - wind_v[1:7] * (old[:, 2:] - old[:, :6])
     new = flow(mid[:, 1:5], wind_u[2:6]) - wind_v[2:6] * (mid[:, 2:] - mid[:, :4])
     for row in range(4):
         put(inner, new[:, row], row, 4)
 
+    after_late = ((me > 0) & (band == 0)) | ((me == 0) & (band == 1))
+    pl.semaphore_wait(
+        barrier,
+        groups - 1 + below.astype(jnp.int32) + above.astype(jnp.int32) - after_late.astype(jnp.int32))
+
+    @pl.when(late)
+    def _():
+        pl.semaphore_signal(band_ready, inc=1, device_id={"lat": band + 1}, device_id_type=MESH)
+
+        def answer(step, carry):
+            pl.semaphore_signal(ready, inc=1, device_id={"member": step}, device_id_type=MESH)
+            return carry
+
+        lax.fori_loop(1, groups, answer, 0)
+
+    @pl.when(above)
+    def _():
+        to_high().start()
+
+    @pl.when(below & jnp.logical_not(after_late))
+    def _():
+        to_low().start()
+
     far_x = [(lax.rem(my_x + dx, SIDE_X)) for dx in FAR_X]
     far_y = [(lax.rem(my_y + dy, SIDE_Y)) for dy in FAR_Y]
     mine = pl.ds(pl.multiple_of(me * 8, 8), 8)
@@ -201,51 +210,14 @@
         for y in far_y:
             tile = x * SIDE_Y + y
 
-            @pl.when((tile > 0) & (2 * tile != me))
+            @pl.when(((tile > 0) | (band > 0)) & (2 * tile != me))
             def _():
                 go(inner, tile, 2 * tile).start()
 
-    @pl.when(below & (me == 0))
+    @pl.when(below & after_late)
     def _():
         pl.semaphore_wait(band_ready, 1)
-        row_down().start()
-
-    first, last = old[:, 0], old[:, 7]
-
-    @pl.when(below)
-    def _():
-        row_up().wait_recv()
-
-    @pl.when(band == 0)
-    def _():
-        low_in[...] = jnp.zeros_like(low_in)
-        low_next[...] = jnp.zeros_like(low_next)
-
-    row0 = flow(first, wind_u[0]) - wind_v[0] * (old[:, 1] - low_in[...])
-    low_out[...] = row0
-
-    @pl.when(below)
-    def _():
-        next_down().start()
-
-    @pl.when(above)
-    def _():
-        row_down().wait_recv()
-
-    @pl.when(band == bands - 1)
-    def _():
-        high_in[...] = jnp.zeros_like(high_in)
-        high_next[...] = jnp.zeros_like(high_next)
-
-    row7 = flow(last, wind_u[7]) - wind_v[7] * (high_in[...] - old[:, 6])
-    high_out[...] = row7
-
-    @pl.when(above)
-    def _():
-        next_up().start()
-
-    put(outer, flow(mid[:, 0], wind_u[1]) - wind_v[1] * (mid[:, 1] - row0), 0, 2)
-    put(outer, flow(mid[:, 5], wind_u[6]) - wind_v[6] * (row7 - mid[:, 4]), 1, 2)
+        to_low().start()
 
     def send_odd(block, near, far):
         for x in far_x:
@@ -256,19 +228,33 @@
                 def _():
                     go(block, x * 2 + slot, peer).start()
 
-    send_odd(outer, 0, 3)
-
     @pl.when(below)
     def _():
-        next_up().wait_recv()
+        to_high().wait_recv()
+
+    @pl.when(band == 0)
+    def _():
+        low_in[...] = jnp.zeros_like(low_in)
+
+    row0 = flow(first, wind_u[0]) - wind_v[0] * (old[:, 1] - low_in[:members])
+    before = low_in[members : 2 * members] - low_in[2 * members] * first
+    put(outer, flow(row0, wind_u[0]) - wind_v[0] * (mid[:, 0] - before), 0, 2)
+    put(outer, flow(mid[:, 0], wind_u[1]) - wind_v[1] * (mid[:, 1] - row0), 1, 2)
+    send_odd(outer, 0, 1)
 
     @pl.when(above)
     def _():
-        next_down().wait_recv()
-
-    put(edge, flow(row0, wind_u[0]) - wind_v[0] * (mid[:, 0] - low_next[...]), 0, 2)
-    put(edge, flow(row7, wind_u[7]) - wind_v[7] * (high_next[...] - mid[:, 5]), 1, 2)
-    send_odd(edge, 1, 2)
+        to_low().wait_recv()
+
+    @pl.when(band == bands - 1)
+    def _():
+        high_in[...] = jnp.zeros_like(high_in)
+
+    row7 = flow(last, wind_u[7]) - wind_v[7] * (high_in[:members] - old[:, 6])
+    after = high_in[members : 2 * members] + high_in[2 * members] * last
+    put(edge, flow(mid[:, 5], wind_u[6]) - wind_v[6] * (row7 - mid[:, 4]), 0, 2)
+    put(edge, flow(row7, wind_u[7]) - wind_v[7] * (after - mid[:, 5]), 1, 2)
+    send_odd(edge, 2, 3)
 
     def keep(block, tile):
         return pltpu.make_async_copy(block.at[pl.ds(pl.multiple_of(tile * 8, 8), 8)], gathered.at[mine], own_sem.at[0])
@@ -277,15 +263,15 @@
     def _():
         keep(inner, index).start()
 
-    @pl.when((odd == 1) & ((my_y == 0) | (my_y == 3)))
-    def _():
-        keep(outer, my_x * 2 + my_y // 3).start()
-
-    @pl.when((odd == 1) & ((my_y == 1) | (my_y == 2)))
-    def _():
-        keep(edge, my_x * 2 + my_y // 2).start()
-
-    @pl.when(me > 0)
+    @pl.when((odd == 1) & (my_y < 2))
+    def _():
+        keep(outer, my_x * 2 + my_y).start()
+
+    @pl.when((odd == 1) & (my_y >= 2))
+    def _():
+        keep(edge, my_x * 2 + my_y - 2).start()
+
+    @pl.when((me > 0) & (band == 0))
     def _():
         pl.semaphore_wait(ready, 1)
         go(inner, 0, 0).start()
@@ -329,7 +315,7 @@
     own.wait()
     pltpu.make_async_copy(returned.at[others], returned.at[others], back_recv).wait()
 
-    for row, place, core in ((2, 0, 0), (3, 1, 0), (4, 2, 0), (5, 3, 0), (1, 0, 1), (0, 1, 1), (7, 2, 1), (6, 3, 1)):
+    for row, place, core in ((2, 0, 0), (3, 1, 0), (4, 2, 0), (5, 3, 0), (0, 0, 1), (1, 1, 1), (6, 2, 1), (7, 3, 1)):
         for half in range(halves):
             for member in range(members):
                 start = (2 * place + core) * 8 + half * members + member
@@ -337,13 +323,11 @@
 
     @pl.when(below)
     def _():
-        row_down().wait_send()
-        next_down().wait_send()
+        to_low().wait_send()
 
     @pl.when(above)
     def _():
-        row_up().wait_send()
-        next_up().wait_send()
+        to_high().wait_send()
 
     pltpu.make_async_copy(gathered.at[others], gathered.at[others], go_send).wait()
     pltpu.make_async_copy(returned.at[others], returned.at[others], back_send).wait()
@@ -356,7 +340,7 @@
     def body(state, zonal, merid, cell, value, weight):
         members, rows, levels, lons = state.shape
         obs = cell.shape[-1]
-        halo = pltpu.VMEM((members, levels, lons), F32)
+        halo = pltpu.VMEM((2 * members + 1, levels, lons), F32)
         tiles = groups * 8
         return pl.pallas_call(
             lambda *refs: kernel(groups, bands, *refs),
@@ -370,7 +354,7 @@
                 pltpu.VMEM((levels, obs), jnp.int32),
                 pltpu.VMEM((levels, obs), F32),
                 pltpu.VMEM((levels, obs), F32),
-                halo, halo, halo, halo, halo, halo,
+                halo, halo, halo, halo,
                 pltpu.VMEM((tiles // 2, LANES), F32),
                 pltpu.VMEM((tiles // 4, LANES), F32),
                 pltpu.VMEM((tiles // 4, LANES), F32),
@@ -378,8 +362,8 @@
                 pltpu.VMEM((tiles, LANES), F32),
                 pltpu.VMEM((tiles, LANES), F32),
                 pltpu.SemaphoreType.DMA((6,)),
-                pltpu.SemaphoreType.DMA((4,)),
-                pltpu.SemaphoreType.DMA((4,)),
+                pltpu.SemaphoreType.DMA((2,)),
+                pltpu.SemaphoreType.DMA((2,)),
                 pltpu.SemaphoreType.DMA,
                 pltpu.SemaphoreType.DMA,
                 pltpu.SemaphoreType.DMA,

time: 44.2 us -> 41.2 us (0.932)
  Pallas kernels: 43.3 us -> 40.3 us
    pallas_call x1, Pallas kernels: 43.3 us -> 40.3 us  [body(): pl.pallas_call(lambda *refs: kernel(groups, bands, *refs), out_shape=pltp...]
where the time goes in v4:
time: 41.2 us; the launch traced here: 41 us
  Pallas kernels  40.3 us (98%)
  local copies, waits for them, and re-layouts  0.71 us (2%)
    pallas_call x1, Pallas kernels, body(): pl.pallas_call(lambda *refs: kernel(groups, bands, *refs), out_shape=pltp...  40.3 us

profile of v4, /device:TPU:769, one launch (start us, length us, event | category | flops | bytes accessed | tf_op | source)
XLA Modules:
  0.0 41.0 jit_solution(815568024859007398)
XLA Ops:
  0.0 40.3 %shard_map.64 = f32[4,8,8,256]{3,2,1,0:T(8,128)S(1)} custom-call(f32[4,8,8,256]{3,2,1,0:T(8,128)} %refs_0_.1, f32[8,8,256]{2,1,0:T(8,128)} %refs_1_.1, f32[8,8,256]{2,1,0:T(8,128)} %refs_2_.1, s32[8,8,128]{2,1,0:T(8,128)} %refs_3_.1, f32[8,8,128]{2,1,0:T(8,128)} %refs_4_.1, f32[8,8,128]{2,1,0:T(8,128)} %refs_5_.1), custom_call_target="tpu_custom_call" | custom-call | tf_op jit(solution)/shard_map/pallas_call | solution.py:345
  40.3 0.7 %copy.8 = f32[4,8,8,256]{3,2,1,0:T(8,128)} copy(f32[4,8,8,256]{3,2,1,0:T(8,128)S(1)} %shard_map.64) | data formatting | bytes 524288

commit v5 on v4

--- a/solution.py
+++ b/solution.py
@@ -48,6 +48,8 @@
     scaled_s = split(scaled)
     turned_s = (scaled_s[0].T, scaled_s[1].T)
     gram = dot3(turned_s, scaled_s)
+    gram_s = split(gram)
+    twice = dot3(gram_s, gram_s)
     cross = dot3(turned_s, pert_s)
     trace = jnp.sum(jnp.sum(scaled * scaled, axis=0, keepdims=True), axis=1, keepdims=True)
     square = jnp.sum(jnp.sum(gram * gram, axis=0, keepdims=True), axis=1, keepdims=True)
@@ -64,7 +66,7 @@
     eye = jnp.where(diagonal, 1.0, 0.0)
     s = gram * unit
     s_s = split(s)
-    s2 = dot3(s_s, s_s)
+    s2 = (twice * unit) * unit
     t2 = (p1 * p1 - a0 * p1) * eye + (0.25 * a0 - p1) * s + 0.25 * s2
     m2 = dot3(s_s, split(t2))
     f2 = p2 * eye - 0.5 * m2
@@ -105,7 +107,9 @@
     halves = lons // LANES
     index, odd = me // 2, me % 2
     my_x, my_y = index // SIDE_Y, index % SIDE_Y
-    my_row = jnp.where(odd == 0, 2 + my_y, my_y + 4 * (my_y // 2))
+    slot = lax.rem(my_y + 2 * (my_x % 2), SIDE_Y)
+    my_row = jnp.where(odd == 0, 2 + my_y, jnp.where(slot < 2, 1 + 5 * slot, 7 * (slot - 2)))
+    home = my_x * 8 + jnp.where(odd == 0, 2 * my_y, 2 * slot + 1)
     my_level = my_x
     below, above = band > 0, band < bands - 1
 
@@ -134,10 +138,11 @@
     @pl.when(jnp.logical_not(late))
     def _():
         def greet(step, carry):
-            pl.semaphore_signal(barrier, inc=1, device_id={"member": lax.rem(me + step, groups)}, device_id_type=MESH)
+            peer = me + 1 + step
+            pl.semaphore_signal(barrier, inc=1, device_id={"member": lax.rem(peer, groups)}, device_id_type=MESH)
             return carry
 
-        lax.fori_loop(1, groups, greet, 0)
+        lax.fori_loop(0, groups - 1, greet, 0)
 
     for load in loads[:3]:
         load.wait()
@@ -153,14 +158,16 @@
     high_out[members : 2 * members] = flow(last, wind_u[7]) + wind_v[7] * old[:, 6]
     high_out[2 * members] = wind_v[7]
 
-    def to_low():
+    raw, rest = pl.ds(0, members), pl.ds(members, members + 1)
+
+    def to_low(number, part):
         return pltpu.make_async_remote_copy(
-            src_ref=low_out, dst_ref=high_in, send_sem=halo_send.at[0], recv_sem=halo_recv.at[0],
+            src_ref=low_out.at[part], dst_ref=high_in.at[part], send_sem=halo_send.at[number], recv_sem=halo_recv.at[number],
             device_id={"lat": band - 1}, device_id_type=MESH)
 
-    def to_high():
+    def to_high(number, part):
         return pltpu.make_async_remote_copy(
-            src_ref=high_out, dst_ref=low_in, send_sem=halo_send.at[1], recv_sem=halo_recv.at[1],
+            src_ref=high_out.at[part], dst_ref=low_in.at[part], send_sem=halo_send.at[number], recv_sem=halo_recv.at[number],
             device_id={"lat": band + 1}, device_id_type=MESH)
 
     def put(block, x, place, every):
@@ -189,15 +196,18 @@
 
         lax.fori_loop(1, groups, answer, 0)
 
-    @pl.when(above)
-    def _():
-        to_high().start()
-
-    @pl.when(below & jnp.logical_not(after_late))
-    def _():
-        to_low().start()
+    for number, part in ((0, raw), (2, rest)):
+
+        @pl.when(above)
+        def _():
+            to_high(number, part).start()
+
+        @pl.when(below & jnp.logical_not(after_late))
+        def _():
+            to_low(number + 1, part).start()
 
     far_x = [(lax.rem(my_x + dx, SIDE_X)) for dx in FAR_X]
+    turned_y = [[2 * lax.rem(slot + 2 * (x % 2), SIDE_Y) for slot in range(4)] for x in far_x]
     far_y = [(lax.rem(my_y + dy, SIDE_Y)) for dy in FAR_Y]
     mine = pl.ds(pl.multiple_of(me * 8, 8), 8)
 
@@ -217,44 +227,53 @@
     @pl.when(below & after_late)
     def _():
         pl.semaphore_wait(band_ready, 1)
-        to_low().start()
-
-    def send_odd(block, near, far):
-        for x in far_x:
-            for slot, y in enumerate((near, far)):
-                peer = x * 8 + 2 * y + 1
+        to_low(1, raw).start()
+        to_low(3, rest).start()
+
+    def send_outer(block, first_slot):
+        for x, turned in zip(far_x, turned_y):
+            for row in range(2):
+                peer = x * 8 + (turned[first_slot + row] + 1)
 
                 @pl.when(peer != me)
                 def _():
-                    go(block, x * 2 + slot, peer).start()
+                    go(block, x * 2 + row, peer).start()
 
     @pl.when(below)
     def _():
-        to_high().wait_recv()
+        to_high(0, raw).wait_recv()
 
     @pl.when(band == 0)
     def _():
         low_in[...] = jnp.zeros_like(low_in)
 
+    @pl.when(above)
+    def _():
+        to_low(1, raw).wait_recv()
+
+    @pl.when(band == bands - 1)
+    def _():
+        high_in[...] = jnp.zeros_like(high_in)
+
     row0 = flow(first, wind_u[0]) - wind_v[0] * (old[:, 1] - low_in[:members])
+    row7 = flow(last, wind_u[7]) - wind_v[7] * (high_in[:members] - old[:, 6])
+    put(outer, flow(mid[:, 0], wind_u[1]) - wind_v[1] * (mid[:, 1] - row0), 0, 2)
+    put(outer, flow(mid[:, 5], wind_u[6]) - wind_v[6] * (row7 - mid[:, 4]), 1, 2)
+    send_outer(outer, 0)
+
+    @pl.when(below)
+    def _():
+        to_high(2, rest).wait_recv()
+
+    @pl.when(above)
+    def _():
+        to_low(3, rest).wait_recv()
+
     before = low_in[members : 2 * members] - low_in[2 * members] * first
-    put(outer, flow(row0, wind_u[0]) - wind_v[0] * (mid[:, 0] - before), 0, 2)
-    put(outer, flow(mid[:, 0], wind_u[1]) - wind_v[1] * (mid[:, 1] - row0), 1, 2)
-    send_odd(outer, 0, 1)
-
-    @pl.when(above)
-    def _():
-        to_low().wait_recv()
-
-    @pl.when(band == bands - 1)
-    def _():
-        high_in[...] = jnp.zeros_like(high_in)
-
-    row7 = flow(last, wind_u[7]) - wind_v[7] * (high_in[:members] - old[:, 6])
     after = high_in[members : 2 * members] + high_in[2 * members] * last
-    put(edge, flow(mid[:, 5], wind_u[6]) - wind_v[6] * (row7 - mid[:, 4]), 0, 2)
+    put(edge, flow(row0, wind_u[0]) - wind_v[0] * (mid[:, 0] - before), 0, 2)
     put(edge, flow(row7, wind_u[7]) - wind_v[7] * (after - mid[:, 5]), 1, 2)
-    send_odd(edge, 2, 3)
+    send_outer(edge, 2)
 
     def keep(block, tile):
         return pltpu.make_async_copy(block.at[pl.ds(pl.multiple_of(tile * 8, 8), 8)], gathered.at[mine], own_sem.at[0])
@@ -263,13 +282,13 @@
     def _():
         keep(inner, index).start()
 
-    @pl.when((odd == 1) & (my_y < 2))
-    def _():
-        keep(outer, my_x * 2 + my_y).start()
-
-    @pl.when((odd == 1) & (my_y >= 2))
-    def _():
-        keep(edge, my_x * 2 + my_y - 2).start()
+    @pl.when((odd == 1) & (slot < 2))
+    def _():
+        keep(outer, my_x * 2 + slot).start()
+
+    @pl.when((odd == 1) & (slot >= 2))
+    def _():
+        keep(edge, my_x * 2 + slot - 2).start()
 
     @pl.when((me > 0) & (band == 0))
     def _():
@@ -293,9 +312,11 @@
             result[pl.ds(half * members + member, groups, stride=8), :] = (
                 analysed[member * groups : (member + 1) * groups, half * LANES : (half + 1) * LANES])
 
+    there = pl.ds(pl.multiple_of(home * 8, 8), 8)
+
     def give(peer):
         return pltpu.make_async_remote_copy(
-            src_ref=result.at[pl.ds(pl.multiple_of(peer * 8, 8), 8)], dst_ref=returned.at[mine],
+            src_ref=result.at[pl.ds(pl.multiple_of(peer * 8, 8), 8)], dst_ref=returned.at[there],
             send_sem=back_send, recv_sem=back_recv, device_id={"member": peer}, device_id_type=MESH)
 
     for x in far_x:
@@ -310,12 +331,12 @@
                 else:
                     give(peer).start()
 
-    own = pltpu.make_async_copy(result.at[mine], returned.at[mine], own_sem.at[1])
+    own = pltpu.make_async_copy(result.at[mine], returned.at[there], own_sem.at[1])
     own.start()
     own.wait()
     pltpu.make_async_copy(returned.at[others], returned.at[others], back_recv).wait()
 
-    for row, place, core in ((2, 0, 0), (3, 1, 0), (4, 2, 0), (5, 3, 0), (0, 0, 1), (1, 1, 1), (6, 2, 1), (7, 3, 1)):
+    for row, place, core in ((2, 0, 0), (3, 1, 0), (4, 2, 0), (5, 3, 0), (1, 0, 1), (6, 1, 1), (0, 2, 1), (7, 3, 1)):
         for half in range(halves):
             for member in range(members):
                 start = (2 * place + core) * 8 + half * members + member
@@ -323,11 +344,13 @@
 
     @pl.when(below)
     def _():
-        to_low().wait_send()
+        to_low(1, raw).wait_send()
+        to_low(3, rest).wait_send()
 
     @pl.when(above)
     def _():
-        to_high().wait_send()
+        to_high(0, raw).wait_send()
+        to_high(2, rest).wait_send()
 
     pltpu.make_async_copy(gathered.at[others], gathered.at[others], go_send).wait()
     pltpu.make_async_copy(returned.at[others], returned.at[others], back_send).wait()
@@ -362,8 +385,8 @@
                 pltpu.VMEM((tiles, LANES), F32),
                 pltpu.VMEM((tiles, LANES), F32),
                 pltpu.SemaphoreType.DMA((6,)),
-                pltpu.SemaphoreType.DMA((2,)),
-                pltpu.SemaphoreType.DMA((2,)),
+                pltpu.SemaphoreType.DMA((4,)),
+                pltpu.SemaphoreType.DMA((4,)),
                 pltpu.SemaphoreType.DMA,
                 pltpu.SemaphoreType.DMA,
                 pltpu.SemaphoreType.DMA,

time: 41.2 us -> 39.8 us (0.966)
  Pallas kernels: 40.3 us -> 38.9 us
    pallas_call x1, Pallas kernels: 40.3 us -> 38.9 us  [body(): pl.pallas_call(lambda *refs: kernel(groups, bands, *refs), out_shape=pltp...]
where the time goes in v5:
time: 39.8 us; the launch traced here: 39.6 us
  Pallas kernels  38.9 us (98%)
  local copies, waits for them, and re-layouts  0.71 us (2%)
    pallas_call x1, Pallas kernels, body(): pl.pallas_call(lambda *refs: kernel(groups, bands, *refs), out_shape=pltp...  38.9 us

profile of v5, /device:TPU:769, one launch (start us, length us, event | category | flops | bytes accessed | tf_op | source)
XLA Modules:
  0.0 39.6 jit_solution(4322628546911766607)
XLA Ops:
  0.0 38.9 %shard_map.64 = f32[4,8,8,256]{3,2,1,0:T(8,128)S(1)} custom-call(f32[4,8,8,256]{3,2,1,0:T(8,128)} %refs_0_.1, f32[8,8,256]{2,1,0:T(8,128)} %refs_1_.1, f32[8,8,256]{2,1,0:T(8,128)} %refs_2_.1, s32[8,8,128]{2,1,0:T(8,128)} %refs_3_.1, f32[8,8,128]{2,1,0:T(8,128)} %refs_4_.1, f32[8,8,128]{2,1,0:T(8,128)} %refs_5_.1), custom_call_target="tpu_custom_call" | custom-call | tf_op jit(solution)/shard_map/pallas_call | solution.py:368
  38.9 0.7 %copy.8 = f32[4,8,8,256]{3,2,1,0:T(8,128)} copy(f32[4,8,8,256]{3,2,1,0:T(8,128)S(1)} %shard_map.64) | data formatting | bytes 524288

commit v6 on v5

--- a/solution.py
+++ b/solution.py
@@ -31,18 +31,22 @@
     return dot(a[0], b[0]) + (dot(a[0], b[1]) + dot(a[1], b[0]))
 
 
-def analyse(ensemble, cells, values, weights):
+def prepare(cells, weights, lons):
+    obs = cells.shape[1]
+    pick = jnp.where(lax.broadcasted_iota(jnp.int32, (lons, obs), 0) == cells, 1.0, 0.0).astype(BF16)
+    diagonal = lax.broadcasted_iota(jnp.int32, (obs, obs), 0) == lax.broadcasted_iota(jnp.int32, (obs, obs), 1)
+    return pick, jnp.sqrt(weights), jnp.where(diagonal, 1.0, 0.0)
+
+
+def analyse(ensemble, values, pick, root_weight, eye):
     count, lons = ensemble.shape
-    obs = cells.shape[1]
     inflate = count - 1.0
     mean = jnp.sum(ensemble, axis=0, keepdims=True) * (1.0 / count)
     pert = ensemble - mean
-    pick = jnp.where(lax.broadcasted_iota(jnp.int32, (lons, obs), 0) == cells, 1.0, 0.0).astype(BF16)
     pert_s = split(pert)
     picked = dot(pert_s[0], pick) + dot(pert_s[1], pick)
     mean_s = split(jnp.broadcast_to(mean, (8, lons)))
     obs_mean = dot(mean_s[0], pick) + dot(mean_s[1], pick)
-    root_weight = jnp.sqrt(weights)
     scaled = picked * root_weight
     target = (values - obs_mean) * root_weight
     scaled_s = split(scaled)
@@ -62,8 +66,6 @@
     q3 = q2 * p2 * p2
     p3 = 1.5 - 0.5 * q3
     z0 = p1 * p2 * p3
-    diagonal = lax.broadcasted_iota(jnp.int32, (obs, obs), 0) == lax.broadcasted_iota(jnp.int32, (obs, obs), 1)
-    eye = jnp.where(diagonal, 1.0, 0.0)
     s = gram * unit
     s_s = split(s)
     s2 = (twice * unit) * unit
@@ -290,14 +292,18 @@
     def _():
         keep(edge, my_x * 2 + slot - 2).start()
 
+    for load in loads[3:]:
+        load.wait()
+    region = pl.ds(my_level, 1)
+    observed = values[region, :]
+    prepared = prepare(cells[region, :], weights[region, :], lons)
+
     @pl.when((me > 0) & (band == 0))
     def _():
         pl.semaphore_wait(ready, 1)
         go(inner, 0, 0).start()
 
     keep(inner, index).wait()
-    for load in loads[3:]:
-        load.wait()
     others = pl.ds(0, (groups - 1) * 8)
     pltpu.make_async_copy(gathered.at[others], gathered.at[others], go_recv).wait()
 
@@ -305,8 +311,7 @@
         [jnp.concatenate(
             [gathered[pl.ds(half * members + member, groups, stride=8), :] for member in range(members)], axis=0)
          for half in range(halves)], axis=1)
-    analysed = analyse(
-        ensemble, cells[pl.ds(my_level, 1), :], values[pl.ds(my_level, 1), :], weights[pl.ds(my_level, 1), :])
+    analysed = analyse(ensemble, observed, *prepared)
     for half in range(halves):
         for member in range(members):
             result[pl.ds(half * members + member, groups, stride=8), :] = (

time: 39.8 us -> 39.8 us (level)
  no operation moved by 1% of the time
where the time goes in v6:
time: 39.8 us; the launch traced here: 39.6 us
  Pallas kernels  38.9 us (98%)
  local copies, waits for them, and re-layouts  0.71 us (2%)
    pallas_call x1, Pallas kernels, body(): pl.pallas_call(lambda *refs: kernel(groups, bands, *refs), out_shape=pltp...  38.9 us

profile of v6, /device:TPU:769, one launch (start us, length us, event | category | flops | bytes accessed | tf_op | source)
XLA Modules:
  0.0 39.6 jit_solution(6148642717307868734)
XLA Ops:
  0.0 38.9 %shard_map.64 = f32[4,8,8,256]{3,2,1,0:T(8,128)S(1)} custom-call(f32[4,8,8,256]{3,2,1,0:T(8,128)} %refs_0_.1, f32[8,8,256]{2,1,0:T(8,128)} %refs_1_.1, f32[8,8,256]{2,1,0:T(8,128)} %refs_2_.1, s32[8,8,128]{2,1,0:T(8,128)} %refs_3_.1, f32[8,8,128]{2,1,0:T(8,128)} %refs_4_.1, f32[8,8,128]{2,1,0:T(8,128)} %refs_5_.1), custom_call_target="tpu_custom_call" | custom-call | tf_op jit(solution)/shard_map/pallas_call | solution.py:373
  38.9 0.7 %copy.8 = f32[4,8,8,256]{3,2,1,0:T(8,128)} copy(f32[4,8,8,256]{3,2,1,0:T(8,128)S(1)} %shard_map.64) | data formatting | bytes 524288
